TPU v7x, 256 devices: a whole 4x4x8 slice. The times are simulated.
256 devices in a mesh: seq: 64 (over z, y, core), grp: 4 (over x).
Axes of the slice: x: 4, y: 4, z: 8, core: 2. Of those that a mesh axis runs over, the one named last changes fastest.
Arguments:
- queries: bfloat16 [65536, 1024], P(('seq', 'grp')), may hold values from -5 to 5
- key_rows: bfloat16 [65536, 128], P(('seq', 'grp')), may hold values from -5 to 5
- value_rows: bfloat16 [65536, 128], P(('seq', 'grp')), may hold values from -6 to 6
- out_grad: bfloat16 [65536, 1024], P(('seq', 'grp')), may hold values from -6 to 6
- segment: int32 [65536], P(('seq', 'grp')), may hold values from 0 to 84, never falling along the last dimension, each value on 1 to 1536 neighbouring positions
Outputs:
- attended: bfloat16 [65536, 1024], P(('seq', 'grp'))
- query_grad: bfloat16 [65536, 1024], P(('seq', 'grp'))
- key_grad: float32 [65536, 128], P(('seq', 'grp'))
- value_grad: float32 [65536, 128], P(('seq', 'grp'))
Inputs may be any that keep to these rules, and one draw needn't show every extreme that they name: `segment`: segment numbers start at 0 and never fall along the sequence; every document holds 1 to 1536 tokens, and one holds exactly 1536.
All inputs are finite; a program needn't handle non-finite values.
Results may differ from a plain program's by a relative error of at most 0.019.
Values may be sent and summed in bfloat16 or wider, within the bound.
No kernel may reach another device: no remote copies, remote signals or barrier semaphores. Data moves between devices by JAX's collectives and lax.ppermute only.
A program may use at most 64 MiB of HBM per device.

v0:
```python
import functools
import math

import jax
import jax.numpy as jnp
from jax import lax
from jax.experimental import pallas as pl
from jax.experimental.pallas import tpu as pltpu
from jax.sharding import PartitionSpec as P

AXES = ("seq", "grp")
NEAR = 3
FAR = 3
NEAR_SIZES = (2, 4)
FAR_SIZES = (0, 1, 3)
GROUP = 8
FAR_MIB = 28
HIDE = -1e30
BF, F32 = jnp.bfloat16, jnp.float32


def wrapped(value, steps, axes=AXES):
    count = lax.axis_size(axes)
    return lax.ppermute(value, axes, [(i, (i + steps) % count) for i in range(count)])


def dot(a, b, over_a, over_b):
    return lax.dot_general(
        a, b, (((over_a,), (over_b,)), ((), ())), preferred_element_type=jnp.float32
    )


def nt(a, b):
    return dot(a, b, 1, 1)


def nn(a, b):
    return dot(a, b, 1, 0)


def tn(a, b):
    return dot(a, b, 0, 0)


def rows(c, size):
    return slice(c * size, (c + 1) * size)


def at(h, size):
    return pl.ds(pl.multiple_of(h * size, size), size)


def marks_of(block, tokens):
    return block[tokens : tokens + 8, :].astype(jnp.float32)


def reached(seg_row, first):
    return jnp.sum(jnp.where(seg_row == first, 1.0, 0.0), axis=1, keepdims=True)


def bias_of(seg_row, row_seg, first, key_at):
    tokens = key_at.shape[0]
    count = reached(seg_row, first)
    shown = (key_at.astype(jnp.float32) >= tokens - count) & (row_seg == first)
    return jnp.where(shown, 0.0, HIDE), jnp.where(count > 0, 1.0, 0.0)


def for_heads(heads, needed, sizes, step, finish=None):
    below = -1
    for size in sizes:

        @pl.when((needed > below) & (needed <= size))
        def _(size=size):
            def group(i, carry):
                step([i * GROUP + k for k in range(GROUP)], size)
                return carry

            lax.fori_loop(0, heads // GROUP, group, 0)
            if finish is not None:
                finish(size)

        below = size


def fold(op, x):
    return op(x.reshape(-1, 8, x.shape[1]), axis=0)


def own_scores(heads, q_ref, own, s_ref, top_ref, qs_ref, bias):
    tokens = q_ref.shape[0]
    width = q_ref.shape[1] // heads
    scale2 = width**-0.5 * math.log2(math.e)
    own_seg = marks_of(own, tokens)
    key_seg = jnp.transpose(own_seg)[:, 0:1]
    key_at = lax.broadcasted_iota(jnp.int32, (tokens, tokens), 0)
    row_at = lax.broadcasted_iota(jnp.int32, (tokens, tokens), 1)
    shown = (key_seg == own_seg[0:1, :]) & (key_at <= row_at)
    bias[...] = jnp.where(shown, 0.0, HIDE)

    def group(i, carry):
        for k in range(GROUP):
            h = i * GROUP + k
            q = q_ref[:, at(h, width)]
            qs_ref[at(h, tokens), :] = q
            s = nt(own[0:tokens, 0:width], q) * scale2 + bias[...]
            s_ref[:, at(h, tokens)] = s
            top_ref[:, at(h, tokens)] = fold(jnp.max, s)
        return carry

    lax.fori_loop(0, heads // GROUP, group, 0)


def near_forward(heads, q_ref, s_ref, top_ref, *refs):
    blocks = refs[: NEAR + 1]
    e_ref, o_ref, stat_ref, ks, vs, bias, *sc = refs[NEAR + 1 :]
    tokens = q_ref.shape[0] // heads
    width = q_ref.shape[1]
    scale2 = width**-0.5 * math.log2(math.e)
    row_seg = marks_of(blocks[0], tokens)[0:1, :]
    key_at = lax.broadcasted_iota(jnp.int32, (tokens, tokens), 0)
    first = row_seg[:, 0:1]
    reach = jnp.ones((1, 1), jnp.float32)
    for c in range(1, NEAR + 1):
        bias[rows(c - 1, tokens), :], more = bias_of(
            marks_of(blocks[c], tokens)[0:1, :], row_seg, first, key_at
        )
        reach = reach + more
    for c in range(NEAR + 1):
        ks[rows(c, tokens), :] = blocks[c][0:tokens, 0:width]
        vs[rows(c, tokens), :] = blocks[c][0:tokens, width : 2 * width]

    def step(hs, size):
        for k, h in enumerate(hs):
            q = q_ref[at(h, tokens), :]
            top = top_ref[:, at(h, tokens)]
            for c in range(1, size):
                r = rows(c - 1, tokens)
                s = nt(ks[rows(c, tokens), :], q) * scale2 + bias[r, :]
                sc[k][r, :] = s
                top = jnp.maximum(top, fold(jnp.max, s))
            top = jnp.max(top, axis=0, keepdims=True)
            total = jnp.zeros((8, tokens), jnp.float32)
            for c in range(size):
                s = sc[k][rows(c - 1, tokens), :] if c else s_ref[:, at(h, tokens)]
                e = jnp.exp2(s - top)
                total = total + fold(jnp.sum, e)
                e_ref[rows(c, tokens), at(h, tokens)] = e.astype(jnp.bfloat16)
            total = jnp.sum(total, axis=0, keepdims=True)
            stat_ref[0:8, at(h, tokens)] = jnp.broadcast_to(top, (8, tokens))
            stat_ref[8:16, at(h, tokens)] = jnp.broadcast_to(total, (8, tokens))
        seen = slice(0, size * tokens)
        for h in hs:
            o_ref[:, at(h, width)] = tn(e_ref[seen, at(h, tokens)], vs[seen, :])

    for_heads(heads, jnp.sum(reach).astype(jnp.int32), NEAR_SIZES, step)


def far_both(heads, q_ref, g_ref, near_out, stat_ref, own, far, *refs):
    o_ref, part, dq_ref, gn_ref, dots_ref, ks, vs, bias, gf, dt, ex, ds, *sc = refs
    tokens = q_ref.shape[0] // heads
    width = q_ref.shape[1]
    scale = width**-0.5
    scale2 = scale * math.log2(math.e)
    pitch = far.shape[0] // FAR
    row_seg = marks_of(own, tokens)[0:1, :]
    first = row_seg[:, 0:1]
    key_at = lax.broadcasted_iota(jnp.int32, (tokens, tokens), 0)
    reach = jnp.zeros((1, 1), jnp.float32)
    for c in range(FAR):
        seg = far[c * pitch + tokens : c * pitch + tokens + 8, :].astype(jnp.float32)[0:1, :]
        bias[rows(c, tokens), :], more = bias_of(seg, row_seg, first, key_at)
        reach = reach + more
        ks[rows(c, tokens), :] = far[c * pitch : c * pitch + tokens, 0:width]
        vs[rows(c, tokens), :] = far[c * pitch : c * pitch + tokens, width : 2 * width]

    def step(hs, size):
        seen = slice(0, size * tokens)
        tops = []
        for k, h in enumerate(hs):
            q = q_ref[at(h, tokens), :]
            top = jnp.broadcast_to(stat_ref[0:1, at(h, tokens)], (8, tokens))
            for c in range(size):
                r = rows(c, tokens)
                s = nt(ks[r, :], q) * scale2 + bias[r, :]
                sc[k][r, :] = s
                top = jnp.maximum(top, fold(jnp.max, s))
            tops.append(jnp.max(top, axis=0, keepdims=True))
        invs = []
        for k, h in enumerate(hs):
            lanes = at(h, tokens)
            top = tops[k]
            keep = jnp.exp2(stat_ref[0:1, lanes] - top)
            total = jnp.zeros((8, tokens), jnp.float32)
            for c in range(size):
                r = rows(c, tokens)
                e = jnp.exp2(sc[k][r, :] - top)
                total = total + fold(jnp.sum, e)
                ex[r, lanes] = e.astype(jnp.bfloat16)
            total = jnp.sum(total, axis=0, keepdims=True) + stat_ref[8:9, lanes] * keep
            inv = 1.0 / total
            invs.append((inv, inv * keep))
        for k, h in enumerate(hs):
            lanes = at(h, tokens)
            inv, near = invs[k]
            both = jnp.concatenate(
                [jnp.broadcast_to(inv, (8, tokens)), jnp.broadcast_to(near, (8, tokens))], axis=0
            )
            cols = jnp.transpose(both)
            inv_rows, near_rows = cols[:, 0:1], cols[:, 8:9]
            g = g_ref[:, at(h, width)].astype(jnp.float32)
            gf[lanes, :] = (g * inv_rows).astype(jnp.bfloat16)
            gn_ref[lanes, :] = (g * near_rows).astype(jnp.bfloat16)
            out = near_out[:, at(h, width)] * near_rows
            if size:
                out = out + tn(ex[seen, lanes], vs[seen, :]) * inv_rows
            o_ref[:, at(h, width)] = out.astype(o_ref.dtype)
            prod = g * out
            high = prod.astype(jnp.bfloat16)
            low = (prod - high.astype(jnp.float32)).astype(jnp.bfloat16)
            ones = jnp.ones((8, width), jnp.bfloat16)
            dots = nt(ones, high) + nt(ones, low)
            dots_ref[:, lanes] = dots * near
            dt[:, lanes] = dots * inv
        if not size:
            return
        for h in hs:
            lanes = at(h, tokens)
            for c in range(size):
                r = rows(c, tokens)
                d = nt(vs[r, :], gf[lanes, :]) - dt[0:1, lanes]
                ds[r, lanes] = (ex[r, lanes].astype(jnp.float32) * d).astype(jnp.bfloat16)
        for h in hs:
            dq_ref[:, at(h, width)] = tn(ds[seen, at(h, tokens)], ks[seen, :])

    def finish(size):
        seen = slice(0, size * tokens)
        if size:
            values = nn(ex[seen, :], gf[...])
            part[seen, width : 2 * width] = values.astype(part.dtype)
            part[seen, 0:width] = (nn(ds[seen, :], q_ref[...]) * scale).astype(part.dtype)
        else:
            dq_ref[...] = jnp.zeros_like(dq_ref)
        if size < FAR:
            part[size * tokens :, :] = jnp.zeros((part.shape[0] - size * tokens, 2 * width), BF)

    for_heads(heads, jnp.sum(reach).astype(jnp.int32), FAR_SIZES, step, finish)


def near_backward(heads, q_ref, gn_ref, dots_ref, e_ref, far_dq, *refs):
    blocks = refs[: NEAR + 1]
    dq_ref, sums, ks, vs, ds = refs[NEAR + 1 :]
    tokens = q_ref.shape[0] // heads
    width = q_ref.shape[1]
    scale = width**-0.5
    row_seg = marks_of(blocks[0], tokens)[0:1, :]
    reach = jnp.ones((1, 1), jnp.float32)
    for c in range(1, NEAR + 1):
        count = reached(marks_of(blocks[c], tokens)[0:1, :], row_seg[:, 0:1])
        reach = reach + jnp.where(count > 0, 1.0, 0.0)
    for c in range(NEAR + 1):
        ks[rows(c, tokens), :] = blocks[c][0:tokens, 0:width]
        vs[rows(c, tokens), :] = blocks[c][0:tokens, width : 2 * width]

    def step(hs, size):
        seen = slice(0, size * tokens)
        for h in hs:
            g = gn_ref[at(h, tokens), :]
            lanes = at(h, tokens)
            for c in range(size):
                r = rows(c, tokens)
                d = nt(vs[r, :], g) - dots_ref[0:1, lanes]
                ds[r, lanes] = (e_ref[r, lanes].astype(jnp.float32) * d).astype(jnp.bfloat16)
        for h in hs:
            lanes = at(h, width)
            dq = far_dq[:, lanes] + tn(ds[seen, at(h, tokens)], ks[seen, :])
            dq_ref[:, lanes] = (dq * scale).astype(dq_ref.dtype)

    def finish(size):
        seen = slice(0, size * tokens)
        sums[seen, width : 2 * width] = nn(e_ref[seen, :], gn_ref[...])
        sums[seen, 0:width] = nn(ds[seen, :], q_ref[...]) * scale
        if size <= NEAR:
            sums[size * tokens :, :] = jnp.zeros((sums.shape[0] - size * tokens, 2 * width), F32)

    for_heads(heads, jnp.sum(reach).astype(jnp.int32), NEAR_SIZES, step, finish)


VM = pl.BlockSpec(memory_space=pltpu.VMEM)


def call(kernel, name, args, outs, scratch, flops, mib):
    return pl.pallas_call(
        kernel,
        out_shape=tuple(jax.ShapeDtypeStruct(*o) for o in outs),
        in_specs=[VM] * len(args),
        out_specs=(VM,) * len(outs),
        scratch_shapes=[pltpu.VMEM(*s) for s in scratch],
        compiler_params=pltpu.CompilerParams(vmem_limit_bytes=mib << 20),
        cost_estimate=pl.CostEstimate(flops=flops, bytes_accessed=1 << 21, transcendentals=0),
        name=name,
    )(*args)


def dims(queries, own):
    tokens = queries.shape[0]
    width = own.shape[1] // 2
    return tokens, width, queries.shape[1] // width


def run_own(queries, own):
    tokens, width, heads = dims(queries, own)
    return call(
        functools.partial(own_scores, heads),
        "own_scores",
        (queries, own),
        [
            ((tokens, heads * tokens), F32),
            ((8, heads * tokens), F32),
            ((heads * tokens, width), BF),
        ],
        [((tokens, tokens), F32)],
        4 * tokens * heads * tokens * width,
        8,
    )


def run_near_forward(stacked, scores, tops, near):
    tokens = near[0].shape[1]
    all_rows, width = stacked.shape
    keys = (NEAR + 1) * tokens
    return call(
        functools.partial(near_forward, all_rows // tokens),
        "near_forward",
        (stacked, scores, tops, *near),
        [((keys, all_rows), BF), ((tokens, all_rows // tokens * width), F32), ((16, all_rows), F32)],
        [((keys, width), BF)] * 2 + [((NEAR * tokens, tokens), F32)] * (1 + GROUP),
        4 * keys * all_rows * width,
        16,
    )


def run_far(stacked, out_grad, near_out, stats, own, far):
    tokens = out_grad.shape[0]
    all_rows, width = stacked.shape
    keys = FAR * tokens
    return call(
        functools.partial(far_both, all_rows // tokens),
        "far_both",
        (stacked, out_grad, near_out, stats, own, far),
        [
            (out_grad.shape, BF),
            ((keys, 2 * width), BF),
            (out_grad.shape, F32),
            ((all_rows, width), BF),
            ((8, all_rows), F32),
        ],
        [((keys, width), BF)] * 2
        + [((keys, tokens), F32), ((all_rows, width), BF), ((8, all_rows), F32)]
        + [((keys, all_rows), BF)] * 2
        + [((keys, tokens), F32)] * GROUP,
        10 * keys * all_rows * width,
        FAR_MIB,
    )


def run_near_backward(stacked, near_grad, dots, weights, far_dq, near):
    tokens = far_dq.shape[0]
    all_rows, width = stacked.shape
    keys = (NEAR + 1) * tokens
    return call(
        functools.partial(near_backward, all_rows // tokens),
        "near_backward",
        (stacked, near_grad, dots, weights, far_dq, *near),
        [(far_dq.shape, BF), ((keys, 2 * width), F32)],
        [((keys, width), BF)] * 2 + [((keys, all_rows), BF)],
        8 * keys * all_rows * width,
        16,
    )


def pack_block(k_hbm, v_hbm, seg_hbm, out, seg, *sems):
    tokens, width = k_hbm.shape
    copies = (
        pltpu.make_async_copy(seg_hbm, seg, sems[0]),
        pltpu.make_async_copy(k_hbm, out.at[0:tokens, 0:width], sems[1]),
        pltpu.make_async_copy(v_hbm, out.at[0:tokens, width : 2 * width], sems[2]),
    )
    for copy in copies:
        copy.start()
    copies[0].wait()
    marks = jnp.broadcast_to(seg[...].astype(jnp.float32), (16, tokens))
    out[tokens : tokens + 16, :] = marks.astype(out.dtype)
    copies[1].wait()
    copies[2].wait()


def run_pack(key_rows, value_rows, segment):
    tokens, width = key_rows.shape
    return pl.pallas_call(
        pack_block,
        out_shape=jax.ShapeDtypeStruct((tokens + 16, 2 * width), BF),
        in_specs=[pl.BlockSpec(memory_space=pl.ANY)] * 3,
        out_specs=VM,
        scratch_shapes=[pltpu.VMEM((1, tokens), jnp.int32)] + [pltpu.SemaphoreType.DMA] * 3,
        compiler_params=pltpu.CompilerParams(vmem_limit_bytes=62 << 20),
        name="pack_block",
    )(key_rows, value_rows, segment.reshape(1, tokens))


def add_parts(sums, far, own, *outs):
    tokens = own.shape[0]
    for d in range(FAR):
        out = outs[d - 1] if d else own
        total = sums[rows(d, tokens), :] + far[rows(d, tokens), :].astype(F32)
        out[...] = total.astype(out.dtype)


def run_add(sums, far):
    one = (far.shape[0] // FAR, far.shape[1])
    outs = [(one, F32)] + [(one, BF)] * (FAR - 1)
    return call(add_parts, "add_parts", (sums, far), outs, [], 1, 4)


def on_device(queries, key_rows, value_rows, out_grad, segment):
    tokens, width = key_rows.shape
    own = run_pack(key_rows, value_rows, segment)
    near = [own] + [wrapped(own, d) for d in range(1, NEAR + 1)]
    near[1:] = lax.optimization_barrier(near[1:])
    far = wrapped(jnp.concatenate(near[:FAR], axis=0), 1, "seq")
    scores, tops, stacked = run_own(queries, own)
    weights, near_out, stats = run_near_forward(stacked, scores, tops, near)
    attended, far_part, far_dq, near_grad, dots = run_far(
        stacked, out_grad, near_out, stats, own, far
    )
    far_back = wrapped(far_part, -1, "seq")
    query_grad, sums = run_near_backward(stacked, near_grad, dots, weights, far_dq, near)
    last = wrapped(sums[NEAR * tokens :].astype(BF), -NEAR)
    total, *parts = run_add(sums, far_back)
    for d, part in enumerate(parts):
        total = total + wrapped(part, -d - 1).astype(F32)
    total = total + last.astype(F32)
    return attended, query_grad, total[:, :width], total[:, width:]


def solution(mesh):
    spec = P(AXES, None)
    return jax.shard_map(
        on_device,
        mesh=mesh,
        in_specs=(spec, spec, spec, spec, P(AXES)),
        out_specs=(spec,) * 4,
        check_vma=False,
    )
```

profile of v0, /device:TPU:128, one launch (start us, length us, event | category | flops | bytes accessed | tf_op | source)
XLA Modules:
  0.0 55.8 jit_solution(10898563513082613581)
XLA Ops:
  0.6 1.6 %pack_block.1.own.refs_0_ = bf16[272,256]{1,0:T(8,128)(2,1)} custom-call(bf16[256,128]{1,0:T(8,128)(2,1)} %k_hbm.1, bf16[256,128]{1,0:T(8,128)(2,1)} %v_hbm.1, s32[1,256]{1,0:T(1,128)} %bitcast.1), custom_call_target="tpu_custom_call" | custom-call | tf_op jit(solution)/shard_map/pack_block/pallas_call | solution.py:399
  2.3 2.8 %collective-permute-start.2 = (bf16[272,256]{1,0:T(8,128)(2,1)}, bf16[272,256]{1,0:T(8,128)(2,1)S(1)}, u32[]{:S(2)}, u32[]{:S(2)}) collective-permute-start(bf16[272,256]{1,0:T(8,128)(2,1)} %pack_block.1.own.refs_0_), channel_id=1, source_target_pairs={{0,3},{1,4},{2,5},{3,6},{4,7},{5,8},{6,9},{7,10},{8,11},{9,12},{10... | collective-permute-start | bytes 417800 | tf_op jit(solution)/shard_map/ppermute | solution.py:24
  5.1 0.4 collective-permute-start.1
  5.5 0.8 %collective-permute-start = (bf16[272,256]{1,0:T(8,128)(2,1)}, bf16[272,256]{1,0:T(8,128)(2,1)S(1)}, u32[]{:S(2)}, u32[]{:S(2)}) collective-permute-start(bf16[272,256]{1,0:T(8,128)(2,1)} %pack_block.1.own.refs_0_), channel_id=1, source_target_pairs={{0,1},{1,2},{2,3},{3,4},{4,5},{5,6},{6,7},{7,8},{8,9},{9,10},{10,1... | collective-permute-start | bytes 417800 | tf_op jit(solution)/shard_map/ppermute | solution.py:24
  6.3 5.1 %collective-permute-done.2.refs_3_ = bf16[272,256]{1,0:T(8,128)(2,1)S(1)} collective-permute-done((bf16[272,256]{1,0:T(8,128)(2,1)}, bf16[272,256]{1,0:T(8,128)(2,1)S(1)}, u32[]{:S(2)}, u32[]{:S(2)}) %collective-permute-start.2) | collective-permute-done | bytes 139296 | tf_op jit(solution)/shard_map/ppermute | solution.py:24
  11.4 5.6 %collective-permute-done.1.refs_2_ = bf16[272,256]{1,0:T(8,128)(2,1)S(1)} collective-permute-done((bf16[272,256]{1,0:T(8,128)(2,1)}, bf16[272,256]{1,0:T(8,128)(2,1)S(1)}, u32[]{:S(2)}, u32[]{:S(2)}) %collective-permute-start.1) | collective-permute-done | bytes 139296 | tf_op jit(solution)/shard_map/ppermute | solution.py:24
  17.0 0.2 collective-permute-done.refs_1_
  17.2 0.9 %pad_maximum_fusion = bf16[816,256]{1,0:T(8,128)(2,1)S(1)} fusion(bf16[272,256]{1,0:T(8,128)(2,1)S(1)} %collective-permute-done.1.refs_2_, bf16[272,256]{1,0:T(8,128)(2,1)S(1)} %collective-permute-done.refs_1_, bf16[272,256]{1,0:T(8,128)(2,1)} %pack_block.1.own.refs_0_), kind=kLoop, calls=%fused_computation | loop fusion | flops 1253376 | bytes 835584 | tf_op jit(solution)/shard_map/concatenate | solution.py:429
  18.1 0.1 collective-permute-start.3
  18.2 0.9 %copy-done = bf16[272,256]{1,0:T(8,128)(2,1)S(1)} copy-done((bf16[272,256]{1,0:T(8,128)(2,1)S(1)}, bf16[272,256]{1,0:T(8,128)(2,1)}, u32[]{:S(2)}) %copy-start) | copy-done | bytes 139288
  19.1 1.0 %copy-done.3 = bf16[256,1024]{1,0:T(8,128)(2,1)S(1)} copy-done((bf16[256,1024]{1,0:T(8,128)(2,1)S(1)}, bf16[256,1024]{1,0:T(8,128)(2,1)}, u32[]{:S(2)}) %copy-start.3) | copy-done | bytes 524312
  20.2 0.5 own_scores.1
  20.7 0.9 %copy-done.1 = bf16[272,256]{1,0:T(8,128)(2,1)S(1)} copy-done((bf16[272,256]{1,0:T(8,128)(2,1)S(1)}, bf16[272,256]{1,0:T(8,128)(2,1)}, u32[]{:S(2)}) %copy-start.1) | copy-done | bytes 139288
  21.6 1.9 %near_forward.1 = (bf16[1024,2048]{1,0:T(8,128)(2,1)S(1)}, f32[256,1024]{1,0:T(8,128)S(1)}, f32[16,2048]{1,0:T(8,128)S(1)}) custom-call(bf16[2048,128]{1,0:T(8,128)(2,1)S(1)} %get-tuple-element.23.q_ref, f32[256,2048]{1,0:T(8,128)S(1)} %get-tuple-element.24.s_ref, f32[8,2048]{1,0:T(8,128)S(1)} %get-tuple-element.25.top_ref, bf16[272,256]{1,0:T(8,128)(2,1)S(1)} %copy-done.1, ...), custom_call_target="tpu_custom_call" | custom-call | flops 1073741824 | bytes 2097152 | tf_op jit(solution)/shard_map/near_forward/pallas_call | solution.py:292
  23.5 5.5 %collective-permute-done.3.far = bf16[816,256]{1,0:T(8,128)(2,1)S(1)} collective-permute-done((bf16[816,256]{1,0:T(8,128)(2,1)S(1)}, bf16[816,256]{1,0:T(8,128)(2,1)S(1)}, u32[]{:S(2)}, u32[]{:S(2)}) %collective-permute-start.3) | collective-permute-done | bytes 417824 | tf_op jit(solution)/shard_map/ppermute | solution.py:24
  29.0 2.3 %far_both.1 = (bf16[256,1024]{1,0:T(8,128)(2,1)}, bf16[768,256]{1,0:T(8,128)(2,1)S(1)}, f32[256,1024]{1,0:T(8,128)S(1)}, bf16[2048,128]{1,0:T(8,128)(2,1)S(1)}, f32[8,2048]{1,0:T(8,128)S(1)}) custom-call(bf16[2048,128]{1,0:T(8,128)(2,1)S(1)} %get-tuple-element.23.q_ref, bf16[256,1024]{1,0:T(8,128)(2,1)S(1)} %copy-done.4, ...), custom_call_target="tpu_custom_call" | custom-call | flops 2013265920 | bytes 2097152 | tf_op jit(solution)/shard_map/far_both/pallas_call | solution.py:292
  31.3 1.7 %collective-permute-start.4 = (bf16[768,256]{1,0:T(8,128)(2,1)S(1)}, bf16[768,256]{1,0:T(8,128)(2,1)S(1)}, u32[]{:S(2)}, u32[]{:S(2)}) collective-permute-start(bf16[768,256]{1,0:T(8,128)(2,1)S(1)} %get-tuple-element.38), channel_id=1, source_target_pairs={{0,252},{4,0},{8,4},{12,8},{16,12},{20,16},{24,20},{28,24},{32,28}... | collective-permute-start | bytes 1179656 | tf_op jit(solution)/shard_map/ppermute | solution.py:24
  33.0 3.7 %near_backward.1 = (bf16[256,1024]{1,0:T(8,128)(2,1)}, f32[1024,256]{1,0:T(8,128)S(1)}) custom-call(bf16[2048,128]{1,0:T(8,128)(2,1)S(1)} %get-tuple-element.23.q_ref, bf16[2048,128]{1,0:T(8,128)(2,1)S(1)} %get-tuple-element.32.gn_ref, f32[8,2048]{1,0:T(8,128)S(1)} %get-tuple-element.33.dots_ref, bf16[1024,2048]{1,0:T(8,128)(2,1)S(1)} %get-tuple-element.34.e_ref, ...), custom_call_target="tpu_custom_call" | custom-call | flops 2147483648 | bytes 2097152 | tf_op jit(solution)/shard_map/near_backward/pallas_call | solution.py:292
  36.7 0.1 collective-permute-start.7
  36.8 1.5 %collective-permute-done.4.far = bf16[768,256]{1,0:T(8,128)(2,1)S(1)} collective-permute-done((bf16[768,256]{1,0:T(8,128)(2,1)S(1)}, bf16[768,256]{1,0:T(8,128)(2,1)S(1)}, u32[]{:S(2)}, u32[]{:S(2)}) %collective-permute-start.4) | collective-permute-done | bytes 393248 | tf_op jit(solution)/shard_map/ppermute | solution.py:24
  38.4 10.2 %collective-permute-start.5 = (bf16[256,256]{1,0:T(8,128)(2,1)S(1)}, bf16[256,256]{1,0:T(8,128)(2,1)S(1)}, u32[]{:S(2)}, u32[]{:S(2)}) collective-permute-start(bf16[256,256]{1,0:T(8,128)(2,1)S(1)} %get-tuple-element.40), channel_id=1, source_target_pairs={{0,255},{1,0},{2,1},{3,2},{4,3},{5,4},{6,5},{7,6},{8,7},{9,8},{10,... | collective-permute-start | bytes 393224 | tf_op jit(solution)/shard_map/ppermute | solution.py:24
  48.6 2.5 %collective-permute-done.5 = bf16[256,256]{1,0:T(8,128)(2,1)S(1)} collective-permute-done((bf16[256,256]{1,0:T(8,128)(2,1)S(1)}, bf16[256,256]{1,0:T(8,128)(2,1)S(1)}, u32[]{:S(2)}, u32[]{:S(2)}) %collective-permute-start.5) | collective-permute-done | bytes 131104 | tf_op jit(solution)/shard_map/ppermute | solution.py:24
  51.1 4.0 %collective-permute-done.6 = bf16[256,256]{1,0:T(8,128)(2,1)S(1)} collective-permute-done((bf16[256,256]{1,0:T(8,128)(2,1)S(1)}, bf16[256,256]{1,0:T(8,128)(2,1)S(1)}, u32[]{:S(2)}, u32[]{:S(2)}) %collective-permute-start.6) | collective-permute-done | bytes 131104 | tf_op jit(solution)/shard_map/ppermute | solution.py:24
  55.1 0.7 %fusion = (f32[256,128]{1,0:T(8,128)}, f32[256,128]{1,0:T(8,128)}) fusion(f32[256,256]{1,0:T(8,128)S(1)} %convert_add_fusion), kind=kLoop, calls=%fused_computation.3 | loop fusion | bytes 524288 | tf_op jit(solution)/shard_map/slice | solution.py:442
  (12 shorter events, 0.2 us)
Async XLA Ops:
  0.6 28.4 %copy-start.4 = (bf16[256,1024]{1,0:T(8,128)(2,1)S(1)}, bf16[256,1024]{1,0:T(8,128)(2,1)}, u32[]{:S(2)}) copy-start(bf16[256,1024]{1,0:T(8,128)(2,1)} %g_ref.1) | copy-start | bytes 1572868
  2.3 26.7 %copy-start.2 = (bf16[272,256]{1,0:T(8,128)(2,1)S(1)}, bf16[272,256]{1,0:T(8,128)(2,1)}, u32[]{:S(2)}) copy-start(bf16[272,256]{1,0:T(8,128)(2,1)} %pack_block.1.own.refs_0_) | copy-start | bytes 417796
  2.3 9.1 %collective-permute-start.2 = (bf16[272,256]{1,0:T(8,128)(2,1)}, bf16[272,256]{1,0:T(8,128)(2,1)S(1)}, u32[]{:S(2)}, u32[]{:S(2)}) collective-permute-start(bf16[272,256]{1,0:T(8,128)(2,1)} %pack_block.1.own.refs_0_), channel_id=1, source_target_pairs={{0,3},{1,4},{2,5},{3,6},{4,7},{5,8},{6,9},{7,10},{8,11},{9,12},{10... | collective-permute-start | bytes 417800 | tf_op jit(solution)/shard_map/ppermute | solution.py:24
  5.1 11.9 %collective-permute-start.1 = (bf16[272,256]{1,0:T(8,128)(2,1)}, bf16[272,256]{1,0:T(8,128)(2,1)S(1)}, u32[]{:S(2)}, u32[]{:S(2)}) collective-permute-start(bf16[272,256]{1,0:T(8,128)(2,1)} %pack_block.1.own.refs_0_), channel_id=1, source_target_pairs={{0,2},{1,3},{2,4},{3,5},{4,6},{5,7},{6,8},{7,9},{8,10},{9,11},{10,... | collective-permute-start | bytes 417800 | tf_op jit(solution)/shard_map/ppermute | solution.py:24
  5.5 11.7 %collective-permute-start = (bf16[272,256]{1,0:T(8,128)(2,1)}, bf16[272,256]{1,0:T(8,128)(2,1)S(1)}, u32[]{:S(2)}, u32[]{:S(2)}) collective-permute-start(bf16[272,256]{1,0:T(8,128)(2,1)} %pack_block.1.own.refs_0_), channel_id=1, source_target_pairs={{0,1},{1,2},{2,3},{3,4},{4,5},{5,6},{6,7},{7,8},{8,9},{9,10},{10,1... | collective-permute-start | bytes 417800 | tf_op jit(solution)/shard_map/ppermute | solution.py:24
  18.1 10.9 %collective-permute-start.3 = (bf16[816,256]{1,0:T(8,128)(2,1)S(1)}, bf16[816,256]{1,0:T(8,128)(2,1)S(1)}, u32[]{:S(2)}, u32[]{:S(2)}) collective-permute-start(bf16[816,256]{1,0:T(8,128)(2,1)S(1)} %pad_maximum_fusion), channel_id=1, source_target_pairs={{0,4},{4,8},{8,12},{12,16},{16,20},{20,24},{24,28},{28,32},{32,36}... | collective-permute-start | bytes 1253384 | tf_op jit(solution)/shard_map/ppermute | solution.py:24
  18.2 0.9 %copy-start = (bf16[272,256]{1,0:T(8,128)(2,1)S(1)}, bf16[272,256]{1,0:T(8,128)(2,1)}, u32[]{:S(2)}) copy-start(bf16[272,256]{1,0:T(8,128)(2,1)} %pack_block.1.own.refs_0_) | copy-start | bytes 417796
  19.1 1.0 %copy-start.3 = (bf16[256,1024]{1,0:T(8,128)(2,1)S(1)}, bf16[256,1024]{1,0:T(8,128)(2,1)}, u32[]{:S(2)}) copy-start(bf16[256,1024]{1,0:T(8,128)(2,1)} %q_ref.1) | copy-start | bytes 1572868
  20.7 0.9 %copy-start.1 = (bf16[272,256]{1,0:T(8,128)(2,1)S(1)}, bf16[272,256]{1,0:T(8,128)(2,1)}, u32[]{:S(2)}) copy-start(bf16[272,256]{1,0:T(8,128)(2,1)} %pack_block.1.own.refs_0_) | copy-start | bytes 417796
  31.3 7.0 %collective-permute-start.4 = (bf16[768,256]{1,0:T(8,128)(2,1)S(1)}, bf16[768,256]{1,0:T(8,128)(2,1)S(1)}, u32[]{:S(2)}, u32[]{:S(2)}) collective-permute-start(bf16[768,256]{1,0:T(8,128)(2,1)S(1)} %get-tuple-element.38), channel_id=1, source_target_pairs={{0,252},{4,0},{8,4},{12,8},{16,12},{20,16},{24,20},{28,24},{32,28}... | collective-permute-start | bytes 1179656 | tf_op jit(solution)/shard_map/ppermute | solution.py:24
  36.7 11.9 %collective-permute-start.7 = (bf16[256,256]{1,0:T(8,128)(2,1)S(1)}, bf16[256,256]{1,0:T(8,128)(2,1)S(1)}, u32[]{:S(2)}, u32[]{:S(2)}) collective-permute-start(bf16[256,256]{1,0:T(8,128)(2,1)S(1)} %slice.17), channel_id=1, source_target_pairs={{0,253},{1,254},{2,255},{3,0},{4,1},{5,2},{6,3},{7,4},{8,5},{9,6},... | collective-permute-start | bytes 393224 | tf_op jit(solution)/shard_map/ppermute | solution.py:24
  38.4 12.7 %collective-permute-start.5 = (bf16[256,256]{1,0:T(8,128)(2,1)S(1)}, bf16[256,256]{1,0:T(8,128)(2,1)S(1)}, u32[]{:S(2)}, u32[]{:S(2)}) collective-permute-start(bf16[256,256]{1,0:T(8,128)(2,1)S(1)} %get-tuple-element.40), channel_id=1, source_target_pairs={{0,255},{1,0},{2,1},{3,2},{4,3},{5,4},{6,5},{7,6},{8,7},{9,8},{10,... | collective-permute-start | bytes 393224 | tf_op jit(solution)/shard_map/ppermute | solution.py:24
  48.6 6.5 %collective-permute-start.6 = (bf16[256,256]{1,0:T(8,128)(2,1)S(1)}, bf16[256,256]{1,0:T(8,128)(2,1)S(1)}, u32[]{:S(2)}, u32[]{:S(2)}) collective-permute-start(bf16[256,256]{1,0:T(8,128)(2,1)S(1)} %get-tuple-element.41), channel_id=1, source_target_pairs={{0,254},{1,255},{2,0},{3,1},{4,2},{5,3},{6,4},{7,5},{8,6},{9,7},{1... | collective-permute-start | bytes 393224 | tf_op jit(solution)/shard_map/ppermute | solution.py:24
where the time goes:
time: 56.4 us; the launch traced here: 55.8 us
  waiting for transfers between devices  24.4 us (43%)
  starting transfers between devices  16.1 us (29%)
  Pallas kernels  10 us (18%)
  local copies, waits for them, and re-layouts  3.59 us (6%)
  other arithmetic  0.99 us (2%)
  between operations  0.73 us (1%)
    ppermute x8, waiting for transfers between devices, wrapped(): lax.ppermute(value, axes, [(i, (i + steps) % count) for i in range(count)])  24.4 us
    ppermute x8, starting transfers between devices, wrapped(): lax.ppermute(value, axes, [(i, (i + steps) % count) for i in range(count)])  16.1 us
    pallas_call x5, Pallas kernels, call(): pl.pallas_call(kernel, out_shape=tuple((jax.ShapeDtypeStruct(*o) for o in...  8.42 us
    unnamed x10, local copies, waits for them, and re-layouts  2.86 us
    pallas_call x1, Pallas kernels, run_pack(): pl.pallas_call(pack_block, out_shape=jax.ShapeDtypeStruct((tokens + 16, 2...  1.63 us
  transfers between devices with their start and end apart: 8, of which 7 were waited for; matrix products, arithmetic and copies ran while one was open for 0% of the time, Pallas kernels for 11%

commit v1 on v0

--- a/solution.py
+++ b/solution.py
@@ -86,7 +86,8 @@
     return op(x.reshape(-1, 8, x.shape[1]), axis=0)
 
 
-def own_scores(heads, q_ref, own, s_ref, top_ref, qs_ref, bias):
+def own_scores(heads, q_ref, own, s_ref, top_ref, qs_ref, held, bias):
+    held[...] = own[...]
     tokens = q_ref.shape[0]
     width = q_ref.shape[1] // heads
     scale2 = width**-0.5 * math.log2(math.e)
@@ -317,6 +318,7 @@
             ((tokens, heads * tokens), F32),
             ((8, heads * tokens), F32),
             ((heads * tokens, width), BF),
+            (own.shape, BF),
         ],
         [((tokens, tokens), F32)],
         4 * tokens * heads * tokens * width,
@@ -424,10 +426,10 @@
 def on_device(queries, key_rows, value_rows, out_grad, segment):
     tokens, width = key_rows.shape
     own = run_pack(key_rows, value_rows, segment)
-    near = [own] + [wrapped(own, d) for d in range(1, NEAR + 1)]
-    near[1:] = lax.optimization_barrier(near[1:])
+    before = [wrapped(own, d) for d in range(1, NEAR + 1)]
+    (scores, tops, stacked, own), before = lax.optimization_barrier((run_own(queries, own), before))
+    near = [own, *before]
     far = wrapped(jnp.concatenate(near[:FAR], axis=0), 1, "seq")
-    scores, tops, stacked = run_own(queries, own)
     weights, near_out, stats = run_near_forward(stacked, scores, tops, near)
     attended, far_part, far_dq, near_grad, dots = run_far(
         stacked, out_grad, near_out, stats, own, far

time: 56.4 us -> 52.6 us (0.933)
  the two profiles are of different devices: /device:TPU:128 before, /device:TPU:64 now
where the time goes in v1:
time: 52.6 us; the launch traced here: 51.9 us
  waiting for transfers between devices  19.1 us (36%)
  Pallas kernels  18 us (34%)
  starting transfers between devices  11.3 us (21%)
  local copies, waits for them, and re-layouts  2.72 us (5%)
  between operations  0.69 us (1%)
    ppermute x8, waiting for transfers between devices, wrapped(): lax.ppermute(value, axes, [(i, (i + steps) % count) for i in range(count)])  19.1 us
    pallas_call x5, Pallas kernels, call(): pl.pallas_call(kernel, out_shape=tuple((jax.ShapeDtypeStruct(*o) for o in...  16.4 us
    ppermute x8, starting transfers between devices, wrapped(): lax.ppermute(value, axes, [(i, (i + steps) % count) for i in range(count)])  11.3 us
    unnamed x6, local copies, waits for them, and re-layouts  1.98 us
    pallas_call x1, Pallas kernels, run_pack(): pl.pallas_call(pack_block, out_shape=jax.ShapeDtypeStruct((tokens + 16, 2...  1.57 us
  transfers between devices with their start and end apart: 8, of which 6 were waited for; matrix products, arithmetic and copies ran while one was open for 0% of the time, Pallas kernels for 21%

profile of v1, /device:TPU:64, one launch (start us, length us, event | category | flops | bytes accessed | tf_op | source)
XLA Modules:
  0.0 51.9 jit_solution(8561535946868792135)
XLA Ops:
  0.6 1.6 %pack_block.1.own = bf16[272,256]{1,0:T(8,128)(2,1)} custom-call(bf16[256,128]{1,0:T(8,128)(2,1)} %k_hbm.1, bf16[256,128]{1,0:T(8,128)(2,1)} %v_hbm.1, s32[1,256]{1,0:T(1,128)} %bitcast.1), custom_call_target="tpu_custom_call" | custom-call | tf_op jit(solution)/shard_map/pack_block/pallas_call | solution.py:401
  2.2 2.8 %collective-permute-start.2 = (bf16[272,256]{1,0:T(8,128)(2,1)}, bf16[272,256]{1,0:T(8,128)(2,1)S(1)}, u32[]{:S(2)}, u32[]{:S(2)}) collective-permute-start(bf16[272,256]{1,0:T(8,128)(2,1)} %pack_block.1.own), channel_id=1, source_target_pairs={{0,3},{1,4},{2,5},{3,6},{4,7},{5,8},{6,9},{7,10},{8,11},{9,12},{10... | collective-permute-start | bytes 417800 | tf_op jit(solution)/shard_map/ppermute | solution.py:24
  5.1 0.4 collective-permute-start.1
  5.4 0.8 %collective-permute-start = (bf16[272,256]{1,0:T(8,128)(2,1)}, bf16[272,256]{1,0:T(8,128)(2,1)S(1)}, u32[]{:S(2)}, u32[]{:S(2)}) collective-permute-start(bf16[272,256]{1,0:T(8,128)(2,1)} %pack_block.1.own), channel_id=1, source_target_pairs={{0,1},{1,2},{2,3},{3,4},{4,5},{5,6},{6,7},{7,8},{8,9},{9,10},{10,1... | collective-permute-start | bytes 417800 | tf_op jit(solution)/shard_map/ppermute | solution.py:24
  6.2 0.9 %copy-done = bf16[272,256]{1,0:T(8,128)(2,1)S(1)} copy-done((bf16[272,256]{1,0:T(8,128)(2,1)S(1)}, bf16[272,256]{1,0:T(8,128)(2,1)}, u32[]{:S(2)}) %copy-start) | copy-done | bytes 139288
  7.1 1.0 %copy-done.1 = bf16[256,1024]{1,0:T(8,128)(2,1)S(1)} copy-done((bf16[256,1024]{1,0:T(8,128)(2,1)S(1)}, bf16[256,1024]{1,0:T(8,128)(2,1)}, u32[]{:S(2)}) %copy-start.1) | copy-done | bytes 524312
  8.2 0.5 own_scores.1
  8.7 2.7 %collective-permute-done.2.refs_3_ = bf16[272,256]{1,0:T(8,128)(2,1)S(1)} collective-permute-done((bf16[272,256]{1,0:T(8,128)(2,1)}, bf16[272,256]{1,0:T(8,128)(2,1)S(1)}, u32[]{:S(2)}, u32[]{:S(2)}) %collective-permute-start.2) | collective-permute-done | bytes 139296 | tf_op jit(solution)/shard_map/ppermute | solution.py:24
  11.3 4.3 %collective-permute-done.1.refs_2_ = bf16[272,256]{1,0:T(8,128)(2,1)S(1)} collective-permute-done((bf16[272,256]{1,0:T(8,128)(2,1)}, bf16[272,256]{1,0:T(8,128)(2,1)S(1)}, u32[]{:S(2)}, u32[]{:S(2)}) %collective-permute-start.1) | collective-permute-done | bytes 139296 | tf_op jit(solution)/shard_map/ppermute | solution.py:24
  15.6 0.6 %collective-permute-done.refs_1_ = bf16[272,256]{1,0:T(8,128)(2,1)S(1)} collective-permute-done((bf16[272,256]{1,0:T(8,128)(2,1)}, bf16[272,256]{1,0:T(8,128)(2,1)S(1)}, u32[]{:S(2)}, u32[]{:S(2)}) %collective-permute-start) | collective-permute-done | bytes 139296 | tf_op jit(solution)/shard_map/ppermute | solution.py:24
  16.3 0.1 collective-permute-start.3
  16.3 4.3 %near_forward.1 = (bf16[1024,2048]{1,0:T(8,128)(2,1)S(1)}, f32[256,1024]{1,0:T(8,128)S(1)}, f32[16,2048]{1,0:T(8,128)S(1)}) custom-call(bf16[2048,128]{1,0:T(8,128)(2,1)S(1)} %get-tuple-element.32.q_ref, f32[256,2048]{1,0:T(8,128)S(1)} %get-tuple-element.33.s_ref, f32[8,2048]{1,0:T(8,128)S(1)} %get-tuple-element.34.top_ref, ...), custom_call_target="tpu_custom_call" | custom-call | flops 1073741824 | bytes 2097152 | tf_op jit(solution)/shard_map/near_forward/pallas_call | solution.py:293
  20.6 5.3 %collective-permute-done.3.far = bf16[816,256]{1,0:T(8,128)(2,1)S(1)} collective-permute-done((bf16[816,256]{1,0:T(8,128)(2,1)S(1)}, bf16[816,256]{1,0:T(8,128)(2,1)S(1)}, u32[]{:S(2)}, u32[]{:S(2)}) %collective-permute-start.3) | collective-permute-done | bytes 417824 | tf_op jit(solution)/shard_map/ppermute | solution.py:24
  25.9 5.3 %far_both.1 = (bf16[256,1024]{1,0:T(8,128)(2,1)}, bf16[768,256]{1,0:T(8,128)(2,1)S(1)}, f32[256,1024]{1,0:T(8,128)S(1)}, bf16[2048,128]{1,0:T(8,128)(2,1)S(1)}, f32[8,2048]{1,0:T(8,128)S(1)}) custom-call(bf16[2048,128]{1,0:T(8,128)(2,1)S(1)} %get-tuple-element.32.q_ref, bf16[256,1024]{1,0:T(8,128)(2,1)S(1)} %copy-done.2, ...), custom_call_target="tpu_custom_call" | custom-call | flops 2013265920 | bytes 2097152 | tf_op jit(solution)/shard_map/far_both/pallas_call | solution.py:293
  31.2 0.0 collective-permute-start.4
  31.2 6.3 %near_backward.1 = (bf16[256,1024]{1,0:T(8,128)(2,1)}, f32[1024,256]{1,0:T(8,128)S(1)}) custom-call(bf16[2048,128]{1,0:T(8,128)(2,1)S(1)} %get-tuple-element.32.q_ref, bf16[2048,128]{1,0:T(8,128)(2,1)S(1)} %get-tuple-element.42.gn_ref, f32[8,2048]{1,0:T(8,128)S(1)} %get-tuple-element.43.dots_ref, bf16[1024,2048]{1,0:T(8,128)(2,1)S(1)} %get-tuple-element.44.e_ref, ...), custom_call_target="tpu_custom_call" | custom-call | flops 2147483648 | bytes 2097152 | tf_op jit(solution)/shard_map/near_backward/pallas_call | solution.py:293
  37.6 0.5 collective-permute-start.7
  38.1 0.1 add_parts.1
  38.1 6.5 %collective-permute-start.5 = (bf16[256,256]{1,0:T(8,128)(2,1)S(1)}, bf16[256,256]{1,0:T(8,128)(2,1)S(1)}, u32[]{:S(2)}, u32[]{:S(2)}) collective-permute-start(bf16[256,256]{1,0:T(8,128)(2,1)S(1)} %get-tuple-element.50), channel_id=1, source_target_pairs={{0,255},{1,0},{2,1},{3,2},{4,3},{5,4},{6,5},{7,6},{8,7},{9,8},{10,... | collective-permute-start | bytes 393224 | tf_op jit(solution)/shard_map/ppermute | solution.py:24
  44.6 0.2 collective-permute-start.6
  44.9 2.3 %collective-permute-done.5 = bf16[256,256]{1,0:T(8,128)(2,1)S(1)} collective-permute-done((bf16[256,256]{1,0:T(8,128)(2,1)S(1)}, bf16[256,256]{1,0:T(8,128)(2,1)S(1)}, u32[]{:S(2)}, u32[]{:S(2)}) %collective-permute-start.5) | collective-permute-done | bytes 131104 | tf_op jit(solution)/shard_map/ppermute | solution.py:24
  47.2 4.0 %collective-permute-done.6 = bf16[256,256]{1,0:T(8,128)(2,1)S(1)} collective-permute-done((bf16[256,256]{1,0:T(8,128)(2,1)S(1)}, bf16[256,256]{1,0:T(8,128)(2,1)S(1)}, u32[]{:S(2)}, u32[]{:S(2)}) %collective-permute-start.6) | collective-permute-done | bytes 131104 | tf_op jit(solution)/shard_map/ppermute | solution.py:24
  51.1 0.1 convert_add_fusion
  51.2 0.7 %fusion = (f32[256,128]{1,0:T(8,128)}, f32[256,128]{1,0:T(8,128)}) fusion(f32[256,256]{1,0:T(8,128)S(1)} %convert_add_fusion), kind=kLoop, calls=%fused_computation.3 | loop fusion | bytes 524288 | tf_op jit(solution)/shard_map/slice | solution.py:444
  (8 shorter events, 0.1 us)
Async XLA Ops:
  2.2 9.1 %collective-permute-start.2 = (bf16[272,256]{1,0:T(8,128)(2,1)}, bf16[272,256]{1,0:T(8,128)(2,1)S(1)}, u32[]{:S(2)}, u32[]{:S(2)}) collective-permute-start(bf16[272,256]{1,0:T(8,128)(2,1)} %pack_block.1.own), channel_id=1, source_target_pairs={{0,3},{1,4},{2,5},{3,6},{4,7},{5,8},{6,9},{7,10},{8,11},{9,12},{10... | collective-permute-start | bytes 417800 | tf_op jit(solution)/shard_map/ppermute | solution.py:24
  5.1 10.6 %collective-permute-start.1 = (bf16[272,256]{1,0:T(8,128)(2,1)}, bf16[272,256]{1,0:T(8,128)(2,1)S(1)}, u32[]{:S(2)}, u32[]{:S(2)}) collective-permute-start(bf16[272,256]{1,0:T(8,128)(2,1)} %pack_block.1.own), channel_id=1, source_target_pairs={{0,2},{1,3},{2,4},{3,5},{4,6},{5,7},{6,8},{7,9},{8,10},{9,11},{10,... | collective-permute-start | bytes 417800 | tf_op jit(solution)/shard_map/ppermute | solution.py:24
  5.4 10.8 %collective-permute-start = (bf16[272,256]{1,0:T(8,128)(2,1)}, bf16[272,256]{1,0:T(8,128)(2,1)S(1)}, u32[]{:S(2)}, u32[]{:S(2)}) collective-permute-start(bf16[272,256]{1,0:T(8,128)(2,1)} %pack_block.1.own), channel_id=1, source_target_pairs={{0,1},{1,2},{2,3},{3,4},{4,5},{5,6},{6,7},{7,8},{8,9},{9,10},{10,1... | collective-permute-start | bytes 417800 | tf_op jit(solution)/shard_map/ppermute | solution.py:24
  6.2 0.9 %copy-start = (bf16[272,256]{1,0:T(8,128)(2,1)S(1)}, bf16[272,256]{1,0:T(8,128)(2,1)}, u32[]{:S(2)}) copy-start(bf16[272,256]{1,0:T(8,128)(2,1)} %pack_block.1.own) | copy-start | bytes 417796
  7.1 1.0 %copy-start.1 = (bf16[256,1024]{1,0:T(8,128)(2,1)S(1)}, bf16[256,1024]{1,0:T(8,128)(2,1)}, u32[]{:S(2)}) copy-start(bf16[256,1024]{1,0:T(8,128)(2,1)} %q_ref.1) | copy-start | bytes 1572868
  8.2 17.7 %copy-start.2 = (bf16[256,1024]{1,0:T(8,128)(2,1)S(1)}, bf16[256,1024]{1,0:T(8,128)(2,1)}, u32[]{:S(2)}) copy-start(bf16[256,1024]{1,0:T(8,128)(2,1)} %g_ref.1) | copy-start | bytes 1572868
  16.3 9.7 %collective-permute-start.3 = (bf16[816,256]{1,0:T(8,128)(2,1)S(1)}, bf16[816,256]{1,0:T(8,128)(2,1)S(1)}, u32[]{:S(2)}, u32[]{:S(2)}) collective-permute-start(bf16[816,256]{1,0:T(8,128)(2,1)S(1)} %pad_maximum_fusion), channel_id=1, source_target_pairs={{0,4},{4,8},{8,12},{12,16},{16,20},{20,24},{24,28},{28,32},{32,36}... | collective-permute-start | bytes 1253384 | tf_op jit(solution)/shard_map/ppermute | solution.py:24
  31.2 6.8 %collective-permute-start.4 = (bf16[768,256]{1,0:T(8,128)(2,1)S(1)}, bf16[768,256]{1,0:T(8,128)(2,1)S(1)}, u32[]{:S(2)}, u32[]{:S(2)}) collective-permute-start(bf16[768,256]{1,0:T(8,128)(2,1)S(1)} %get-tuple-element.48), channel_id=1, source_target_pairs={{0,252},{4,0},{8,4},{12,8},{16,12},{20,16},{24,20},{28,24},{32,28}... | collective-permute-start | bytes 1179656 | tf_op jit(solution)/shard_map/ppermute | solution.py:24
  37.6 7.3 %collective-permute-start.7 = (bf16[256,256]{1,0:T(8,128)(2,1)S(1)}, bf16[256,256]{1,0:T(8,128)(2,1)S(1)}, u32[]{:S(2)}, u32[]{:S(2)}) collective-permute-start(bf16[256,256]{1,0:T(8,128)(2,1)S(1)} %slice.17), channel_id=1, source_target_pairs={{0,253},{1,254},{2,255},{3,0},{4,1},{5,2},{6,3},{7,4},{8,5},{9,6},... | collective-permute-start | bytes 393224 | tf_op jit(solution)/shard_map/ppermute | solution.py:24
  38.1 9.0 %collective-permute-start.5 = (bf16[256,256]{1,0:T(8,128)(2,1)S(1)}, bf16[256,256]{1,0:T(8,128)(2,1)S(1)}, u32[]{:S(2)}, u32[]{:S(2)}) collective-permute-start(bf16[256,256]{1,0:T(8,128)(2,1)S(1)} %get-tuple-element.50), channel_id=1, source_target_pairs={{0,255},{1,0},{2,1},{3,2},{4,3},{5,4},{6,5},{7,6},{8,7},{9,8},{10,... | collective-permute-start | bytes 393224 | tf_op jit(solution)/shard_map/ppermute | solution.py:24
  44.6 6.5 %collective-permute-start.6 = (bf16[256,256]{1,0:T(8,128)(2,1)S(1)}, bf16[256,256]{1,0:T(8,128)(2,1)S(1)}, u32[]{:S(2)}, u32[]{:S(2)}) collective-permute-start(bf16[256,256]{1,0:T(8,128)(2,1)S(1)} %get-tuple-element.51), channel_id=1, source_target_pairs={{0,254},{1,255},{2,0},{3,1},{4,2},{5,3},{6,4},{7,5},{8,6},{9,7},{1... | collective-permute-start | bytes 393224 | tf_op jit(solution)/shard_map/ppermute | solution.py:24
